TPU v7x, 32 devices: a whole 2x2x4 slice. The times are simulated.
32 devices in a mesh: row: 16 (over z, y, x), col: 2 (over core).
Axes of the slice: x: 2, y: 2, z: 4, core: 2. Of those that a mesh axis runs over, the one named last changes fastest.
Arguments:
- w_integral: bfloat16 [38400, 4800], P('row', 'col'), may hold values from -0.125 to 0.125
- amplitudes: bfloat16 [4800, 4800], P('row', 'col'), may hold values from -6 to 6
- task_tiles: int32 [16, 7], P('row'), may hold values from -1 to 7, as said below
Outputs:
- residual: bfloat16 [38400, 4800], P('row', 'col')
Inputs may be any that keep to these rules, and one draw needn't show every extreme that they name: `task_tiles`: in each row block the live entries come first, name distinct contraction tiles, and number 1 to 7; the remaining entries are -1. Some row block has 7 live entries, and row blocks 2 m and 2 m + 1 together have exactly 8.
All inputs are finite; a program needn't handle non-finite values.
Results may differ from a plain program's by a relative error of at most 0.001.
Values may be sent and summed in bfloat16 or wider, within the bound.
A program may use at most 128 MiB of HBM per device.

v0:
```python
import jax
import jax.numpy as jnp
from jax import lax
from jax.sharding import PartitionSpec as P

TILE = 24
OCC_BLK = 25
KT = 8


def body(w_integral, amplitudes, task_tiles):
    row_panel = lax.all_gather(w_integral, "col", axis=1, tiled=True)
    tile_width = OCC_BLK * TILE
    own_list = task_tiles[0]
    tile_ids = jnp.arange(KT, dtype=jnp.int32)
    live_tiles = jnp.sum((own_list[:, None] == tile_ids[None, :]).astype(jnp.int32), axis=0)
    live_columns = jnp.repeat(live_tiles, tile_width).astype(jnp.bfloat16)
    masked = row_panel * live_columns[None, :]
    cycle_term = jnp.dot(
        masked,
        lax.all_gather(amplitudes, "row", axis=0, tiled=True),
        preferred_element_type=jnp.float32,
    )
    return cycle_term.astype(jnp.bfloat16)


def solution(mesh):
    placed = (P("row", "col"), P("row", "col"), P("row", None))
    return jax.shard_map(
        body, mesh=mesh, in_specs=placed, out_specs=P("row", "col"), check_vma=False
    )
```

profile of v0, /device:TPU:0, one launch (start us, length us, event | category | flops | bytes accessed | tf_op | source)
XLA Modules:
  0.0 398.7 jit_solution(16415654778048669757)
XLA Ops:
  6.5 0.0 copy-start
  6.5 0.0 all-gather.6.cloned.1.call-start
  6.5 0.7 all-gather.6.cloned.1.call-update
  7.3 0.0 all-gather.4.cloned.1.call-start
  7.3 16.7 %copy.5 = bf16[2400,2400]{0,1:T(8,128)(2,1)} copy(bf16[2400,2400]{1,0:T(8,128)(2,1)} %param.3) | data formatting | bytes 23040000 | tf_op args[0]
  24.0 0.0 all-gather.4.cloned.1.call-update
  24.1 0.0 copy-done
  24.1 0.1 convert_reduce_fusion
  24.2 0.1 broadcast_in_dim.2
  24.2 0.1 convert_element_type.19
  24.3 245.3 %all-gather.6.cloned.1.call-done = bf16[16,300,2400]{2,1,0:T(8,128)(2,1)} async-done(((bf16[1,300,2400]{2,1,0:T(8,128)(2,1)}), bf16[16,300,2400]{2,1,0:T(8,128)(2,1)}) %all-gather.6.cloned.1.call-update) | async-done | bytes 23040016 | tf_op jit(solution)/shard_map/all_gather | solution.py:21
  269.6 24.2 %reshape.9 = bf16[4800,2400]{1,0:T(8,128)(2,1)} reshape(bf16[16,300,2400]{2,1,0:T(8,128)(2,1)} %all-gather.6.cloned.1.call-done) | data formatting | bytes 46080000
  293.8 13.8 %all-gather.4.cloned.1.call-done = bf16[2400,4800]{0,1:T(8,128)(2,1)} async-done(((bf16[2400,2400]{0,1:T(8,128)(2,1)}), bf16[2400,4800]{0,1:T(8,128)(2,1)}) %all-gather.4.cloned.1.call-update) | async-done | bytes 23040016 | tf_op jit(solution)/shard_map/all_gather | solution.py:12
  307.6 84.2 %fusion.2 = bf16[2400,2400]{1,0:T(8,128)(2,1)} fusion(bf16[4800,2400]{1,0:T(8,128)(2,1)} %reshape.9, bf16[2400,4800]{0,1:T(8,128)(2,1)} %all-gather.4.cloned.1.call-done, bf16[4800]{0:T(1024)(128)(2,1)S(1)} %convert_element_type.19), kind=kOutput, calls=%fused_computation.2 | convolution fusion | flops 55313276928 | bytes 57609600 | tf_op jit(solution)/shard_map/dot_general | solution.py:19
  (1 shorter events, 0.0 us)
Async XLA Ops:
  6.5 17.5 %copy-start = (s32[1,7]{1,0:T(1,128)S(1)}, s32[1,7]{1,0:T(1,128)}, u32[]{:S(2)}) copy-start(s32[1,7]{1,0:T(1,128)} %param.5) | copy-start | bytes 88
  6.5 263.1 %all-gather.6.cloned.1.call-start = ((), (), s32[]{:S(2)}) async-start(), calls=%async_computation.1 | async-start | bytes 25137152 | tf_op jit(solution)/shard_map/all_gather | solution.py:21
  7.3 300.3 %all-gather.4.cloned.1.call-start = ((), (), s32[]{:S(2)}) async-start(), calls=%async_computation | async-start | bytes 35020800 | tf_op jit(solution)/shard_map/all_gather | solution.py:12
Sparse Core Ops, SparseCore 0:
  10.1 259.5 all-gather.5
  271.2 36.3 all-gather.3
where the time goes:
time: 399 us
  waiting for transfers between devices  260 us (65%)
  matrix products  84.2 us (21%)
  local copies, waits for them, and re-layouts  41.1 us (10%)
  between operations  13.4 us (3%)
    all_gather x1, waiting for transfers between devices, body(): lax.all_gather(amplitudes, 'row', axis=0, tiled=True)  245 us
    dot_general x1, matrix products, body(): jnp.dot(masked, lax.all_gather(amplitudes, 'row', axis=0, tiled=True), pr...  84.2 us
    unnamed x4, local copies, waits for them, and re-layouts  40.9 us
    all_gather x1, waiting for transfers between devices, body(): row_panel = lax.all_gather(w_integral, 'col', axis=1, tiled=True)  13.8 us
  transfers between devices with their start and end apart: 2, of which 2 were waited for; matrix products, arithmetic and copies ran while one was open for 10% of the time, Pallas kernels for 0%

commit v1 on v0

v1 whole, which is shorter than its diff:
```python
import functools

import jax
import jax.numpy as jnp
from jax import lax
from jax.experimental import pallas as pl
from jax.experimental.pallas import tpu as pltpu
from jax.sharding import PartitionSpec as P

KT = 8
PIECES = 6
MESH = pl.DeviceIdType.MESH
XD, YD, ZUP, ZDN = 0, 1, 2, 3


def kernel(n, cols, cfg, w_ref, t_ref, live_ref, out_ref, wt_ref,
           tbuf, acc, win, wout, wbuf, obuf,
           recv_sem, send_sem, own_sem, win_sem, wl_sem, ws_sem, wr_sem, wb_sem, o_sem):
    rows, kw, width, kshard, spad, group, chunk, bounds, splits = cfg
    nchunk = rows // chunk
    tiles = kw // (kshard * group)
    zs_count = n // 4
    me = lax.axis_index("row")
    col = lax.axis_index("col")
    x = lax.rem(me, 2)
    y = lax.rem(me // 2, 2)
    z = me // 4
    xo, yo = 1 - x, 1 - y
    far = jnp.where(2 * z < zs_count, zs_count - 1, 0)

    def idx(zz, yy, xx):
        return (zz * 2 + yy) * 2 + xx

    target = [(idx(z, y, xo), col), (idx(z, yo, x), col),
              (idx(z + 1, y, x), col), (idx(z - 1, y, x), col)]
    has_up, has_dn = z + 1 < zs_count, z > 0

    barrier = pltpu.get_barrier_semaphore()

    def greet(dev):
        pl.semaphore_signal(barrier, inc=1, device_id=dev, device_id_type=MESH)

    greet(target[XD])
    greet(target[YD])
    pl.when(has_up)(lambda: greet(target[ZUP]))
    pl.when(has_dn)(lambda: greet(target[ZDN]))
    for o in range(1, cols):
        greet((me, lax.rem(col + o, cols)))
    heard = 1 + cols + jnp.where(has_up, 1, 0) + jnp.where(has_dn, 1, 0)
    own = pltpu.make_async_copy(t_ref, tbuf.at[me], own_sem)
    own.start()
    own.wait()
    pl.semaphore_wait(barrier, heard)

    def piece(shard, p):
        return tbuf.at[shard, pl.ds(bounds[p], bounds[p + 1] - bounds[p])]

    def remote(link, shard, p):
        return pltpu.make_async_remote_copy(
            src_ref=piece(shard, p), dst_ref=piece(shard, p),
            send_sem=send_sem.at[link, shard, p], recv_sem=recv_sem.at[shard, p],
            device_id=target[link], device_id_type=MESH)

    def send(go, link, shard, p):
        if go:
            remote(link, shard, p).start()
        else:
            remote(link, shard, p).wait_send()

    def arrive(go, shard, p):
        if go:
            remote(XD, shard, p).wait_recv()

    half = PIECES // 2
    via_z = list(range(1, PIECES - 1))
    via_x, via_y = PIECES - 1, 0

    def own_stage(go):
        for p in range(PIECES):
            send(go, XD, me, p)
            send(go, YD, me, p)
            pl.when(has_up)(functools.partial(send, go, ZUP, me, p))
            pl.when(has_dn)(functools.partial(send, go, ZDN, me, p))

    def onward(go, d, shard, p):
        pl.when((d > 0) & has_dn)(functools.partial(send, go, ZDN, shard, p))
        pl.when((d < 0) & has_up)(functools.partial(send, go, ZUP, shard, p))

    def both(k, work):
        def step(i, carry):
            d = 1 - 2 * i
            zz = z + d * k

            @pl.when((zz >= 0) & (zz < zs_count))
            def _():
                work(d, zz)
            return carry
        lax.fori_loop(0, 2, step, 0)

    def line_stage(go, k):
        def work(d, zz):
            s = idx(zz, y, x)
            for p in range(PIECES):
                arrive(go, s, p)
                onward(go, d, s, p)
                send(go, XD, s, p)
                send(go, YD, s, p)
        both(k, work)

    def diag_stage(go, k):
        def work(d, zz):
            s = idx(zz, yo, xo)
            for p in via_z:
                arrive(go, s, p)
                onward(go, d, s, p)
        both(k, work)

    def side(go, zz, to_y, to_x):
        sx, sy = idx(zz, y, xo), idx(zz, yo, x)
        for p in range(PIECES):
            arrive(go, sx, p)
            if p in to_y:
                send(go, YD, sx, p)
            arrive(go, sy, p)
            if p in to_x:
                send(go, XD, sy, p)

    def side_stage(go, k):
        both(k, lambda d, zz: side(go, zz, (via_y,), (via_x,)))

    def diag_home(go):
        s = idx(z, yo, xo)
        for p in range(PIECES):
            arrive(go, s, p)
            if p in via_z:
                pl.when(has_up)(functools.partial(send, go, ZUP, s, p))
                pl.when(has_dn)(functools.partial(send, go, ZDN, s, p))

    home = (tuple(range(half)), tuple(range(half, PIECES)))

    own_stage(True)

    wout[...] = jnp.zeros_like(wout)

    def w_in(c, slot):
        return pltpu.make_async_copy(w_ref.at[pl.ds(c * chunk, chunk)], win.at[slot], win_sem.at[slot])

    def w_dst(c, owner):
        return wt_ref.at[pl.ds(owner * tiles, tiles), pl.ds(c * chunk, chunk)]

    def w_local(c, slot):
        return pltpu.make_async_copy(wout.at[slot], w_dst(c, col), wl_sem.at[slot])

    def w_remote(c, slot, o):
        return pltpu.make_async_remote_copy(
            src_ref=wout.at[slot], dst_ref=w_dst(c, col),
            send_sem=ws_sem.at[slot, o], recv_sem=wr_sem.at[c, o],
            device_id=(me, lax.rem(col + o, cols)), device_id_type=MESH)

    def w_drain(c, slot):
        w_local(c, slot).wait()
        for o in range(1, cols):
            w_remote(c, slot, o).wait_send()

    w_in(0, 0).start()

    def w_step(c, carry):
        slot = lax.rem(c, 2)
        pl.when(c + 1 < nchunk)(lambda: w_in(c + 1, 1 - slot).start())
        w_in(c, slot).wait()
        pl.when(c >= 2)(lambda: w_drain(c - 2, slot))
        for j in range(tiles):
            for g in range(group):
                at = (j * group + g) * kshard
                wout[slot, j, :, g * spad:g * spad + kshard] = win[slot, :, at:at + kshard]
        w_local(c, slot).start()
        for o in range(1, cols):
            w_remote(c, slot, o).start()
        return carry

    lax.fori_loop(0, nchunk, w_step, 0)

    def w_wait():
        for c in range(max(0, nchunk - 2), nchunk):
            w_drain(c, c % 2)

        def step(c, carry):
            for o in range(1, cols):
                pltpu.make_async_remote_copy(
                    src_ref=wout.at[0], dst_ref=w_dst(c, lax.rem(col + cols - o, cols)),
                    send_sem=ws_sem.at[0, o], recv_sem=wr_sem.at[c, o],
                    device_id=(me, lax.rem(col + o, cols)), device_id_type=MESH).wait_recv()
            return carry
        lax.fori_loop(0, nchunk, step, 0)

    def product(first_shard, kind):
        t = first_shard // group
        live = live_ref[t]

        def fetch(c, slot):
            return pltpu.make_async_copy(wt_ref.at[t, pl.ds(c * chunk, chunk)], wbuf.at[slot], wb_sem.at[slot])

        def store(c, slot):
            return pltpu.make_async_copy(obuf.at[slot], out_ref.at[pl.ds(c * chunk, chunk)], o_sem.at[slot])

        fetch(0, 0).start()

        def step(c, carry):
            slot = lax.rem(c, 2)
            pl.when(c + 1 < nchunk)(lambda: fetch(c + 1, 1 - slot).start())
            fetch(c, slot).wait()
            if kind == "last":
                pl.when(c >= 2)(lambda: store(c - 2, slot).wait())
            a = wbuf[slot]
            at = pl.ds(pl.multiple_of(c * chunk, 16), chunk)
            for lo, hi in splits:
                b = tbuf[pl.ds(t * group, group), :, lo:hi].reshape(group * spad, hi - lo)
                d = jnp.dot(a, b, preferred_element_type=jnp.float32) * live
                if kind == "first":
                    acc[at, lo:hi] = d
                elif kind == "last":
                    obuf[slot, :, lo:hi] = (acc[at, lo:hi] + d).astype(jnp.bfloat16)
                else:
                    acc[at, lo:hi] += d
            if kind == "last":
                store(c, slot).start()
            return carry

        lax.fori_loop(0, nchunk, step, 0)
        if kind == "last":
            for c in range(max(0, nchunk - 2), nchunk):
                store(c, c % 2).wait()

    pair = group == 2

    line_stage(True, 1)
    side(True, z, *home)
    w_wait()
    if pair:
        product(idx(z, y, 0), "first")
        diag_home(True)
        product(idx(z, yo, 0), "add")
    else:
        diag_home(True)
        product(idx(z, 0, 0), "first")

    def loop(k, carry):
        line_stage(True, k)
        diag_stage(True, k - 1)
        side_stage(True, k - 1)

        def finish(d, zz):
            if pair:
                product(idx(zz, y, 0), "add")
            s = idx(zz, yo, xo)
            for p in (via_x, via_y):
                arrive(True, s, p)

            @pl.when(zz != far)
            def _():
                product(idx(zz, yo if pair else 0, 0), "add")
        both(k - 1, finish)
        return carry

    lax.fori_loop(2, zs_count + 1, loop, 0)
    product(idx(far, yo if pair else 0, 0), "last")

    own_stage(False)
    side(False, z, *home)
    diag_home(False)

    def drain(k, carry):
        line_stage(False, k)
        diag_stage(False, k)
        side_stage(False, k)
        return carry
    lax.fori_loop(1, zs_count, drain, 0)


def body(n, cols, w, t, task_tiles):
    rows, kw = w.shape
    kshard, width = t.shape
    depth = kshard * n // KT
    group = depth // kshard
    spad = -(-kshard // 16) * 16
    chunk = max(c for c in range(16, min(rows, 240) + 1, 16) if rows % c == 0)
    units = spad // 16
    bounds = tuple(units * p // PIECES * 16 for p in range(PIECES + 1))
    parts = max(1, width // 768)
    edges = [768 * i for i in range(parts)] + [width]
    splits = tuple(zip(edges[:-1], edges[1:]))
    tiles = kw // depth
    nchunk = rows // chunk
    tile_ids = jnp.arange(KT, dtype=jnp.int32)
    live = jnp.sum((task_tiles[0][:, None] == tile_ids[None, :]).astype(jnp.int32), axis=0)
    t = jnp.pad(t, ((0, spad - kshard), (0, 0)))
    cfg = (rows, kw, width, kshard, spad, group, chunk, bounds, splits)
    any_space = pl.BlockSpec(memory_space=pl.ANY)
    bf16 = jnp.bfloat16
    out, _ = pl.pallas_call(
        functools.partial(kernel, n, cols, cfg),
        out_shape=(jax.ShapeDtypeStruct((rows, width), bf16),
                   jax.ShapeDtypeStruct((KT, rows, group * spad), bf16)),
        in_specs=[any_space, any_space, pl.BlockSpec(memory_space=pltpu.SMEM)],
        out_specs=(any_space, any_space),
        scratch_shapes=[
            pltpu.VMEM((n, spad, width), bf16),
            pltpu.VMEM((rows, width), jnp.float32),
            pltpu.VMEM((2, chunk, kw), bf16),
            pltpu.VMEM((2, tiles, chunk, group * spad), bf16),
            pltpu.VMEM((2, chunk, group * spad), bf16),
            pltpu.VMEM((2, chunk, width), bf16),
            pltpu.SemaphoreType.DMA((n, PIECES)),
            pltpu.SemaphoreType.DMA((4, n, PIECES)),
            pltpu.SemaphoreType.DMA,
            pltpu.SemaphoreType.DMA((2,)),
            pltpu.SemaphoreType.DMA((2,)),
            pltpu.SemaphoreType.DMA((2, cols)),
            pltpu.SemaphoreType.DMA((nchunk, cols)),
            pltpu.SemaphoreType.DMA((2,)),
            pltpu.SemaphoreType.DMA((2,)),
        ],
        compiler_params=pltpu.CompilerParams(
            collective_id=0, has_side_effects=True, vmem_limit_bytes=62 * 1024 * 1024),
        cost_estimate=pl.CostEstimate(
            flops=2 * rows * width * depth * KT, bytes_accessed=8 * rows * width, transcendentals=0),
    )(w, t, live.astype(jnp.float32))
    return out


def solution(mesh):
    placed = (P("row", "col"), P("row", "col"), P("row", None))
    return jax.shard_map(
        functools.partial(body, mesh.shape["row"], mesh.shape["col"]),
        mesh=mesh, in_specs=placed, out_specs=P("row", "col"), check_vma=False)
```

time: 399 us -> 273 us (0.68)
  waiting for transfers between devices: 260 us -> 0 us
  Pallas kernels: 0 us -> 258 us
  matrix products: 84.2 us -> 0 us
  local copies, waits for them, and re-layouts: 41.1 us -> 12.5 us
  between operations: 13.4 us -> 0.01 us
    all_gather x2 -> x0, waiting for transfers between devices: 259 us -> none  [the longest x1 245 us: body(): lax.all_gather(amplitudes, 'row', axis=0, tiled=True)]
    pallas_call x0 -> x1, Pallas kernels: none -> 258 us  [body(): pl.pallas_call(functools.partial(kernel, n, cols, cfg), out_shape=(jax.Sh...]
    dot_general x1 -> x0, matrix products: 84.2 us -> none  [body(): jnp.dot(masked, lax.all_gather(amplitudes, 'row', axis=0, tiled=True), pr...]
    unnamed x4 -> x1, local copies, waits for them, and re-layouts: 40.9 us -> 9.95 us
  transfers between devices with their start and end apart: 2 -> 0, of which waited for: 2 -> 0; matrix products, arithmetic and copies ran while one was open for 10% -> 0% of each run, Pallas kernels for 0% -> 0%
where the time goes in v1:
time: 273 us; the launch traced here: 272 us
  Pallas kernels  258 us (95%)
  local copies, waits for them, and re-layouts  12.5 us (5%)
    pallas_call x1, Pallas kernels, body(): pl.pallas_call(functools.partial(kernel, n, cols, cfg), out_shape=(jax.Sh...  258 us
    unnamed x1, local copies, waits for them, and re-layouts  9.95 us

profile of v1, /device:TPU:0, one launch (start us, length us, event | category | flops | bytes accessed | tf_op | source)
XLA Modules:
  0.0 271.9 jit_solution(5729393608801308309)
XLA Ops:
  0.0 0.7 convert_reduce_fusion
  0.7 0.5 convert_element_type.9.live_ref
  1.3 2.6 pad.4.t_ref
  3.9 258.1 %shard_map.37 = (bf16[2400,2400]{1,0:T(8,128)(2,1)}, bf16[8,2400,608]{2,1,0:T(8,128)(2,1)}) custom-call(bf16[2400,2400]{1,0:T(8,128)(2,1)} %w_ref.1, bf16[304,2400]{1,0:T(8,128)(2,1)} %pad.4.t_ref, f32[8]{0:T(128)} %convert_element_type.9.live_ref), custom_call_target="tpu_custom_call" | custom-call | flops 55296000000 | bytes 46080000 | tf_op jit(solution)/shard_map/pallas_call | solution.py:300
  262.0 10.0 %copy.5 = bf16[2400,2400]{1,0:T(8,128)(2,1)} copy(bf16[2400,2400]{1,0:T(8,128)(2,1)} %get-tuple-element.6) | data formatting | bytes 23040000

commit v2 on v1

--- a/solution.py
+++ b/solution.py
@@ -1,4 +1,6 @@
 import functools
+import heapq
+import itertools
 
 import jax
 import jax.numpy as jnp
@@ -9,8 +11,70 @@
 
 KT = 8
 PIECES = 6
+STRETCH = 0.16
+BURST = 4
 MESH = pl.DeviceIdType.MESH
 XD, YD, ZUP, ZDN = 0, 1, 2, 3
+
+
+def plan(zs_count, group, nchunk, bounds):
+    half = PIECES // 2
+    dur = [(b - a) / bounds[-1] for a, b in zip(bounds[:-1], bounds[1:])]
+    latency = 0.04
+
+    def routes(z, y, x, zz, yy, xx, p):
+        outs = []
+        onward = [s for s in (-1, 1) if 0 <= z + s < zs_count and s * (z - zz) >= 0]
+        if (y, x) == (yy, xx):
+            outs = onward + ["x", "y"]
+        elif y == yy:
+            outs = ["y"] if (p < half if z == zz else p == 0) else []
+        elif x == xx:
+            outs = ["x"] if (p >= half if z == zz else p == PIECES - 1) else []
+        elif 0 < p < PIECES - 1:
+            outs = onward
+        return outs
+
+    devices = list(itertools.product(range(zs_count), range(2), range(2)))
+    count, events, free = itertools.count(), [], {}
+    arrivals = {z: [] for z in range(zs_count)}
+    for d in devices:
+        for p in range(PIECES):
+            heapq.heappush(events, (0.0, next(count), d, d, p))
+    while events:
+        now, _, d, s, p = heapq.heappop(events)
+        z, y, x = d
+        outs = routes(*d, *s, p)
+        if d != s and (y, x) == (0, 0):
+            arrivals[z].append((now, s, p, tuple(outs)))
+        for link in outs:
+            end = max(now, free.get((d, link), 0.0)) + dur[p]
+            free[d, link] = end
+            to = (z, y, 1 - x) if link == "x" else (z, 1 - y, x) if link == "y" else (z + link, y, x)
+            heapq.heappush(events, (end + latency, next(count), to, s, p))
+    total = max(a[-1][0] for a in arrivals.values()) + 1e-6
+    stretches = int(-(-total // STRETCH))
+    order, tiles, ready = [], [], []
+    for z in range(zs_count):
+        cut = [[] for _ in range(stretches)]
+        done = {}
+        for now, s, p, outs in arrivals[z]:
+            cut[int(now // STRETCH)].append((s, p, outs))
+            key = (s[0], s[1] if group == 2 else 0)
+            done[key] = max(done.get(key, 0), int(now // STRETCH))
+        order.append(cut)
+        by_time = sorted(done, key=lambda k: (done[k], abs(k[0] - z), k))
+        tiles.append(by_time)
+        ready.append([done[k] for k in by_time])
+    inner = (KT - 1) * nchunk
+    marks = []
+    for z in range(zs_count):
+        reached = [0]
+        for k in range(stretches):
+            here = nchunk * sum(r <= k for r in ready[z])
+            reached.append(min(here, reached[-1] + BURST, inner))
+        marks.append(reached)
+    return order, tiles, stretches, marks, inner
 
 
 def kernel(n, cols, cfg, w_ref, t_ref, live_ref, out_ref, wt_ref,
@@ -26,7 +90,6 @@
     y = lax.rem(me // 2, 2)
     z = me // 4
     xo, yo = 1 - x, 1 - y
-    far = jnp.where(2 * z < zs_count, zs_count - 1, 0)
 
     def idx(zz, yy, xx):
         return (zz * 2 + yy) * 2 + xx
@@ -193,77 +256,87 @@
             return carry
         lax.fori_loop(0, nchunk, step, 0)
 
-    def product(first_shard, kind):
-        t = first_shard // group
+    order, tile_order, stretches, marks, inner = plan(zs_count, group, nchunk, bounds)
+    total = KT * nchunk
+
+    def tile_at(i):
+        t = 0
+        for zi in range(zs_count):
+            for k, (tz, ty) in enumerate(tile_order[zi]):
+                own_y = jnp.where(y == 0, ty, 1 - ty)
+                value = tz * 2 + own_y if group == 2 else tz
+                t = jnp.where((z == zi) & (i == k), value, t)
+        return t
+
+    def fetch(q):
+        slot = lax.rem(q, 2)
+        return pltpu.make_async_copy(
+            wt_ref.at[tile_at(q // nchunk), pl.ds(lax.rem(q, nchunk) * chunk, chunk)],
+            wbuf.at[slot], wb_sem.at[slot])
+
+    def store(c, slot):
+        return pltpu.make_async_copy(obuf.at[slot], out_ref.at[pl.ds(c * chunk, chunk)], o_sem.at[slot])
+
+    def product(last, q, carry):
+        slot, c = lax.rem(q, 2), lax.rem(q, nchunk)
+        t = tile_at(q // nchunk)
         live = live_ref[t]
-
-        def fetch(c, slot):
-            return pltpu.make_async_copy(wt_ref.at[t, pl.ds(c * chunk, chunk)], wbuf.at[slot], wb_sem.at[slot])
-
-        def store(c, slot):
-            return pltpu.make_async_copy(obuf.at[slot], out_ref.at[pl.ds(c * chunk, chunk)], o_sem.at[slot])
-
-        fetch(0, 0).start()
-
-        def step(c, carry):
-            slot = lax.rem(c, 2)
-            pl.when(c + 1 < nchunk)(lambda: fetch(c + 1, 1 - slot).start())
-            fetch(c, slot).wait()
-            if kind == "last":
-                pl.when(c >= 2)(lambda: store(c - 2, slot).wait())
-            a = wbuf[slot]
-            at = pl.ds(pl.multiple_of(c * chunk, 16), chunk)
-            for lo, hi in splits:
-                b = tbuf[pl.ds(t * group, group), :, lo:hi].reshape(group * spad, hi - lo)
-                d = jnp.dot(a, b, preferred_element_type=jnp.float32) * live
-                if kind == "first":
-                    acc[at, lo:hi] = d
-                elif kind == "last":
-                    obuf[slot, :, lo:hi] = (acc[at, lo:hi] + d).astype(jnp.bfloat16)
-                else:
-                    acc[at, lo:hi] += d
-            if kind == "last":
-                store(c, slot).start()
-            return carry
-
-        lax.fori_loop(0, nchunk, step, 0)
-        if kind == "last":
-            for c in range(max(0, nchunk - 2), nchunk):
-                store(c, c % 2).wait()
-
-    pair = group == 2
-
-    line_stage(True, 1)
-    side(True, z, *home)
+        pl.when(q + 1 < total)(lambda: fetch(q + 1).start())
+        fetch(q).wait()
+        oslot = lax.rem(c, 2)
+        if last:
+            pl.when(c >= 2)(lambda: store(c - 2, oslot).wait())
+        a = wbuf[slot]
+        at = pl.ds(pl.multiple_of(c * chunk, 16), chunk)
+        for lo, hi in splits:
+            b = tbuf[pl.ds(t * group, group), :, lo:hi].reshape(group * spad, hi - lo)
+            d = jnp.dot(a, b, preferred_element_type=jnp.float32) * live
+            if last:
+                obuf[oslot, :, lo:hi] = (acc[at, lo:hi] + d).astype(jnp.bfloat16)
+            else:
+                acc[at, lo:hi] += d
+        if last:
+            store(c, oslot).start()
+        return carry
+
+    def clear(c, carry):
+        acc[pl.ds(pl.multiple_of(c * chunk, 16), chunk), :] = jnp.zeros((chunk, width), jnp.float32)
+        return carry
+
+    lax.fori_loop(0, nchunk, clear, 0)
     w_wait()
-    if pair:
-        product(idx(z, y, 0), "first")
-        diag_home(True)
-        product(idx(z, yo, 0), "add")
-    else:
-        diag_home(True)
-        product(idx(z, 0, 0), "first")
-
-    def loop(k, carry):
-        line_stage(True, k)
-        diag_stage(True, k - 1)
-        side_stage(True, k - 1)
-
-        def finish(d, zz):
-            if pair:
-                product(idx(zz, y, 0), "add")
-            s = idx(zz, yo, xo)
-            for p in (via_x, via_y):
-                arrive(True, s, p)
-
-            @pl.when(zz != far)
+    fetch(0).start()
+
+    def relay(events):
+        for (sz, sy, sx), p, outs in events:
+            shard = idx(sz, y if sy == 0 else yo, x if sx == 0 else xo)
+            arrive(True, shard, p)
+            for link in outs:
+                send(True, {"x": XD, "y": YD, 1: ZUP, -1: ZDN}[link], shard, p)
+
+    def stretch(k, carry):
+        for zi in range(zs_count):
+            @pl.when(z == zi)
             def _():
-                product(idx(zz, yo if pair else 0, 0), "add")
-        both(k - 1, finish)
+                for ki in range(stretches):
+                    if order[zi][ki]:
+                        pl.when(k == ki)(functools.partial(relay, order[zi][ki]))
+        lax.fori_loop(mark(k), mark(k + 1), functools.partial(product, False), 0)
         return carry
 
-    lax.fori_loop(2, zs_count + 1, loop, 0)
-    product(idx(far, yo if pair else 0, 0), "last")
+    def mark(k):
+        value = 0
+        for zi in range(zs_count):
+            for ki, m in enumerate(marks[zi]):
+                if m:
+                    value = jnp.where((z == zi) & (k == ki), m, value)
+        return value
+
+    lax.fori_loop(0, stretches, stretch, 0)
+    lax.fori_loop(mark(stretches), inner, functools.partial(product, False), 0)
+    lax.fori_loop(inner, total, functools.partial(product, True), 0)
+    for c in range(max(0, nchunk - 2), nchunk):
+        store(c, c % 2).wait()
 
     own_stage(False)
     side(False, z, *home)

time: 273 us -> 222 us (0.81)
  the two profiles are of different devices: /device:TPU:0 before, /device:TPU:16 now
where the time goes in v2:
time: 222 us
  Pallas kernels  208 us (94%)
  local copies, waits for them, and re-layouts  12.5 us (6%)
    pallas_call x1, Pallas kernels, body(): pl.pallas_call(functools.partial(kernel, n, cols, cfg), out_shape=(jax.Sh...  208 us
    unnamed x1, local copies, waits for them, and re-layouts  9.95 us

profile of v2, /device:TPU:16, one launch (start us, length us, event | category | flops | bytes accessed | tf_op | source)
XLA Modules:
  0.0 221.8 jit_solution(1489935666061812999)
XLA Ops:
  0.0 0.7 convert_reduce_fusion
  0.7 0.5 convert_element_type.9.live_ref
  1.3 2.6 %pad.4.t_ref = bf16[304,2400]{1,0:T(8,128)(2,1)} pad(bf16[300,2400]{1,0:T(8,128)(2,1)} %param.4, bf16[]{:T(256)} %constant.2.clone.1), padding=0_4x0_0 | pad | bytes 2899202 | tf_op jit(solution)/shard_map/jit(_pad)/pad | solution.py:369
  3.9 208.0 %shard_map.37 = (bf16[2400,2400]{1,0:T(8,128)(2,1)}, bf16[8,2400,608]{2,1,0:T(8,128)(2,1)}) custom-call(bf16[2400,2400]{1,0:T(8,128)(2,1)} %w_ref.1, bf16[304,2400]{1,0:T(8,128)(2,1)} %pad.4.t_ref, f32[8]{0:T(128)} %convert_element_type.9.live_ref), custom_call_target="tpu_custom_call" | custom-call | flops 55296000000 | bytes 46080000 | tf_op jit(solution)/shard_map/pallas_call | solution.py:373
  211.9 10.0 %copy.5 = bf16[2400,2400]{1,0:T(8,128)(2,1)} copy(bf16[2400,2400]{1,0:T(8,128)(2,1)} %get-tuple-element.6) | data formatting | bytes 23040000
